TPU v7x, 256 devices: a whole 4x4x8 slice. The times are simulated.
256 devices in a mesh: chan: 32 (over z, y_lo, core), tm: 8 (over y_hi, x).
Axes of the slice: x: 4, y: 4 (y_hi: 2, y_lo: 2; y = y_hi * 2 + y_lo), z: 8, core: 2. Of those that a mesh axis runs over, the one named last changes fastest.
Arguments:
- record: float32 [16384, 16384], P('tm', 'chan'), may hold values from -6 to 6
- coefficients: float32 [128, 2, 32, 16384], P('tm', None, 'chan'), may hold values from -3 to 3
- band_start: int32 [1], replicated, may hold values from 1 to 97
- band_level: int32 [32], replicated, may hold values from 0 to 7
- levels: float32 [8], replicated, may hold values from 0.3 to 2
Outputs:
- updated: float32 [128, 2, 32, 16384], P('tm', None, 'chan')
- residual: float32 [16384, 16384], P('tm', 'chan')
Inputs may be any that keep to these rules, and one draw needn't show every extreme that they name: The band's bins band_start to band_start + 31 lie at or below bin 256 / 2.
All inputs are finite; a program needn't handle non-finite values.
Results may differ from a plain program's by a relative error of at most 0.000082.
Values sent between devices are 32-bit elements; how exact they have to be, the bound alone decides.
A program may use at most 192 MiB of HBM per device.

v0:
```python
import functools
import math

import jax
import jax.numpy as jnp
import ml_dtypes
import numpy as np
from jax import lax
from jax.experimental import pallas as pl
from jax.experimental.pallas import tpu as pltpu
from jax.sharding import PartitionSpec as P

FRAME = 256
HOP = 128
NB = 32
CHUNK = 4
MESH = pl.DeviceIdType.MESH
F32 = jnp.float32
BF16 = jnp.bfloat16


def halves_of(table):
    high = table.astype(ml_dtypes.bfloat16)
    low = (table - high.astype(np.float64)).astype(ml_dtypes.bfloat16)
    return np.stack([high, low])


def dft_tables(devices):
    side = 128
    idx = np.arange(side)
    angle = 2.0 * math.pi * (np.outer(idx, idx) % side) / side
    c, s = np.cos(angle), np.sin(angle)
    inverse = np.block([[c, -s], [s, c]])
    per = side // devices
    order = [r * side + d * per + q for d in range(devices) for r in range(2) for q in range(per)]
    first = inverse
    second = inverse[order]
    turn = 2.0 * math.pi * np.outer(idx, idx) / side**2
    twist = np.stack([np.cos(turn), np.sin(turn)]).astype(np.float32) / np.float32(side)
    return halves_of(first), halves_of(second), halves_of(second.T), halves_of(first.T), twist


def window_table():
    n = np.arange(HOP)[:, None] + np.where(np.arange(4 * NB)[None] < 2 * NB, HOP, 0)
    return (np.sin((n + 0.5) * (math.pi / FRAME)) / math.sqrt(FRAME)).astype(np.float32)


def split(x):
    high = x.astype(BF16)
    return high, (x - high.astype(F32)).astype(BF16)


def dot3(matrix, x, transposed=False):
    high, low = split(x)
    dims = (((1,), (1 if transposed else 0,)), ((), ()))
    dot = functools.partial(lax.dot_general, dimension_numbers=dims, preferred_element_type=F32)
    return dot(matrix[0], high) + (dot(matrix[0], low) + dot(matrix[1], high))


def kernel(
    n_chan, n_tm,
    start_ref, level_ref, levels_ref, coef_hbm, rec_hbm, first_ref, second_ref, back1_ref, back2_ref, twist_ref, window_ref, windowt_ref,
    upd_hbm, res_hbm,
    coef, rec, send_f, recv_f, send_b, recv_b, halo_s, halo_p, send_p, carry, synth, analy,
    in_sem, out_sem, ssem_f, rsem_f, ssem_b, rsem_b, hsend, hrecv,
):
    me = lax.axis_index("chan")
    t = lax.axis_index("tm")
    before, after = lax.rem(t + n_tm - 1, n_tm), lax.rem(t + 1, n_tm)
    frames = coef.shape[0]
    chunks = frames // CHUNK
    side = 128

    load_coef = pltpu.make_async_copy(coef_hbm, coef, in_sem.at[0])
    load_rec = pltpu.make_async_copy(rec_hbm, rec, in_sem.at[1])
    load_coef.start()
    load_rec.start()

    barrier = pltpu.get_barrier_semaphore()

    def greet(i, _):
        pl.semaphore_signal(barrier, inc=1, device_id={"chan": lax.rem(me + i, n_chan)}, device_id_type=MESH)
        return 0

    lax.fori_loop(1, n_chan, greet, 0)
    for other in (before, after):
        pl.semaphore_signal(barrier, inc=1, device_id={"tm": other}, device_id_type=MESH)

    def forward(j):
        for pair in range(CHUNK // 2):
            q = j * CHUNK + 2 * pair
            lanes = [coef[lax.rem(q + a + frames - 1, frames)] for a in range(2)]
            y = dot3(first_ref, jnp.concatenate(lanes, axis=1))
            rows = []
            for a in range(2):
                yr, yi = y[:side, a * side:(a + 1) * side], y[side:, a * side:(a + 1) * side]
                tr = yr * twist_ref[0] - yi * twist_ref[1]
                ti = yr * twist_ref[1] + yi * twist_ref[0]
                rows.append(jnp.concatenate([tr, ti], axis=1))
            x = dot3(second_ref, jnp.concatenate(rows, axis=0), True)
            for a in range(2):
                send_f[j, 2 * pair + a] = x[:, a * side:(a + 1) * side]

    def exchange(src, dst, ssem, rsem, j):
        mine = pl.ds(pl.multiple_of(me * 8, 8), 8)

        def one(i, _):
            d = lax.rem(me + i, n_chan)
            pltpu.make_async_remote_copy(
                src_ref=src.at[j, :, pl.ds(pl.multiple_of(d * 8, 8), 8)],
                dst_ref=dst.at[j, :, mine],
                send_sem=ssem.at[j],
                recv_sem=rsem.at[j],
                device_id={"chan": d},
                device_id_type=MESH,
            ).start()
            return 0

        lax.fori_loop(1, n_chan, one, 0)
        pltpu.make_async_copy(src.at[j, :, mine], dst.at[j, :, mine], rsem.at[j]).start()

    def wait_bytes(ref, sem):
        pltpu.make_async_copy(ref, ref, sem).wait()

    load_coef.wait()
    forward(0)
    pl.semaphore_wait(barrier, n_chan + 1)
    exchange(send_f, recv_f, ssem_f, rsem_f, 0)

    def forward_step(j, _):
        forward(j)
        exchange(send_f, recv_f, ssem_f, rsem_f, j)
        return 0

    lax.fori_loop(1, chunks, forward_step, 0)

    start = start_ref[0]

    def wave(n_axis, window):
        n_idx = lax.broadcasted_iota(jnp.int32, (side, side), n_axis)
        col = lax.broadcasted_iota(jnp.int32, (side, side), 1 - n_axis)
        later = jnp.where(col < 2 * NB, HOP, 0)
        within = col & (2 * NB - 1)
        phase = ((n_idx + later) * (start + (within >> 1)) + (within & 1) * (FRAME // 4)) & (FRAME - 1)
        return window * jnp.cos(phase.astype(F32) * (2.0 * math.pi / FRAME))

    synth[0], synth[1] = split(2.0 * wave(0, window_ref[...]))
    analy[0], analy[1] = split(wave(1, windowt_ref[...]))
    carry[...] = jnp.zeros_like(carry)
    load_rec.wait()

    def spectra(i, tile):
        q = lax.rem(i + 1, frames)
        return recv_f[q // CHUNK, lax.rem(q, CHUNK), pl.ds(tile, 2 * NB, stride=4)]

    def residual_half(i, h, own, following):
        cols = slice(h * 256, (h + 1) * 256)
        est = dot3(synth, jnp.concatenate([jnp.concatenate(own, axis=1), jnp.concatenate(following, axis=1)], axis=0))
        rest = rec[i, :, cols] - est
        rec[i, :, cols] = rest
        return dot3(analy, rest)

    def put(i, tile, value, add=False):
        p = lax.rem(i + frames - 2, frames)
        where = (p // CHUNK, lax.rem(p, CHUNK), pl.ds(tile, 2 * NB, stride=4))
        send_b[where] = value + send_b[where] if add else value

    def store_residual(i):
        pltpu.make_async_copy(rec.at[i], res_hbm.at[i], out_sem.at[0]).start()

    def step(i, _):
        for h in range(2):
            cols = slice(h * 256, (h + 1) * 256)
            tiles = (2 * h, 2 * h + 1)
            part = residual_half(i, h, [spectra(i, k) for k in tiles], [spectra(i + 1, k) for k in tiles])
            analysed = part[:2 * NB] + carry[:, cols]
            carry[:, cols] = part[2 * NB:]
            for a, k in enumerate(tiles):
                put(i, k, analysed[:, a * side:(a + 1) * side])
        store_residual(i)
        return 0

    wait_bytes(recv_f.at[0], rsem_f.at[0])
    halo_out = pltpu.make_async_remote_copy(
        src_ref=recv_f.at[0, 1], dst_ref=halo_s, send_sem=hsend.at[0], recv_sem=hrecv.at[0],
        device_id={"tm": before}, device_id_type=MESH)
    halo_out.start()
    lax.fori_loop(0, CHUNK - 2, step, 0)

    def middle(j):
        wait_bytes(recv_f.at[j], rsem_f.at[j])
        lax.fori_loop(j * CHUNK - 2, j * CHUNK + 2, step, 0)
        exchange(send_b, recv_b, ssem_b, rsem_b, j - 1)

    middle(1)

    halo_out.wait()
    last = frames - 1
    for h in range(2):
        tiles = (2 * h, 2 * h + 1)
        following = [jnp.where(t < n_tm - 1, halo_s[pl.ds(k, 2 * NB, stride=4)], 0.0) for k in tiles]
        part = residual_half(last, h, [spectra(last, k) for k in tiles], following)
        send_p[:, h * 256:(h + 1) * 256] = part[2 * NB:]
        for a, k in enumerate(tiles):
            put(last, k, part[:2 * NB, a * side:(a + 1) * side])
    store_residual(last)
    part_out = pltpu.make_async_remote_copy(
        src_ref=send_p, dst_ref=halo_p, send_sem=hsend.at[1], recv_sem=hrecv.at[1],
        device_id={"tm": after}, device_id_type=MESH)
    part_out.start()

    def middle_step(j, _):
        middle(j)
        return 0

    lax.fori_loop(2, chunks, middle_step, 0)
    step(frames - 2, 0)
    part_out.wait()
    for k in range(4):
        cols = slice(k * side, (k + 1) * side)
        put(last, k, carry[:, cols], True)
        put(0, k, jnp.where(t > 0, halo_p[:, cols], 0.0), True)
    exchange(send_b, recv_b, ssem_b, rsem_b, chunks - 1)

    limit = levels_ref[level_ref[me]]

    def backward(j, _):
        wait_bytes(recv_b.at[j], rsem_b.at[j])
        for pair in range(CHUNK // 2):
            y = dot3(back1_ref, jnp.concatenate([recv_b[j, 2 * pair], recv_b[j, 2 * pair + 1]], axis=1))
            rows = []
            for a in range(2):
                yr, yi = y[:side, a * side:(a + 1) * side], y[side:, a * side:(a + 1) * side]
                tr = yr * twist_ref[0] + yi * twist_ref[1]
                ti = yi * twist_ref[0] - yr * twist_ref[1]
                rows.append(jnp.concatenate([tr, ti], axis=1))
            u = dot3(back2_ref, jnp.concatenate(rows, axis=0), True)
            for a in range(2):
                f = lax.rem(j * CHUNK + 2 * pair + a + 2, frames)
                cr = coef[f, :side] + u[:side, a * side:(a + 1) * side]
                ci = coef[f, side:] + u[side:, a * side:(a + 1) * side]
                m = jnp.sqrt(cr * cr + ci * ci)
                shrink = jnp.maximum(m - limit, 0.0) / jnp.maximum(m, limit)
                coef[f, :side] = cr * shrink
                coef[f, side:] = ci * shrink
                pltpu.make_async_copy(coef.at[f], upd_hbm.at[f], out_sem.at[1]).start()
        return 0

    lax.fori_loop(0, chunks, backward, 0)

    def drain(j, _):
        for buf, sem in ((send_f, ssem_f), (send_b, ssem_b)):
            wait_bytes(buf.at[j, :, pl.ds(0, 8 * (n_chan - 1))], sem.at[j])
        return 0

    lax.fori_loop(0, chunks, drain, 0)
    wait_bytes(rec, out_sem.at[0])
    wait_bytes(coef, out_sem.at[1])


def body(n_chan, n_tm, record, coefficients, band_start, band_level, levels):
    rows, cols = record.shape
    frames = coefficients.shape[0]
    chunks = frames // CHUNK
    window = window_table()
    tables = [jnp.asarray(x) for x in (*dft_tables(n_chan), window, window.T.copy())]
    vmem, smem, hbm = (pl.BlockSpec(memory_space=m) for m in (pltpu.VMEM, pltpu.SMEM, pl.ANY))
    block = pltpu.VMEM((chunks, CHUNK, 8 * n_chan, 128), F32)
    updated, residual = pl.pallas_call(
        functools.partial(kernel, n_chan, n_tm),
        out_shape=(jax.ShapeDtypeStruct((frames, 256, 128), F32), jax.ShapeDtypeStruct((frames, HOP, cols), F32)),
        in_specs=[smem] * 3 + [hbm] * 2 + [vmem] * len(tables),
        out_specs=(hbm, hbm),
        scratch_shapes=[
            pltpu.VMEM((frames, 256, 128), F32),
            pltpu.VMEM((frames, HOP, cols), F32),
            block, block, block, block,
            pltpu.VMEM((8 * n_chan, 128), F32),
            pltpu.VMEM((2 * NB, cols), F32),
            pltpu.VMEM((2 * NB, cols), F32),
            pltpu.VMEM((2 * NB, cols), F32),
            pltpu.VMEM((2, 128, 128), BF16),
            pltpu.VMEM((2, 128, 128), BF16),
            pltpu.SemaphoreType.DMA((2,)),
            pltpu.SemaphoreType.DMA((2,)),
            pltpu.SemaphoreType.DMA((chunks,)),
            pltpu.SemaphoreType.DMA((chunks,)),
            pltpu.SemaphoreType.DMA((chunks,)),
            pltpu.SemaphoreType.DMA((chunks,)),
            pltpu.SemaphoreType.DMA((2,)),
            pltpu.SemaphoreType.DMA((2,)),
        ],
        compiler_params=pltpu.CompilerParams(
            collective_id=0, has_side_effects=True, vmem_limit_bytes=48 * 1024 * 1024
        ),
    )(
        band_start, band_level, levels,
        coefficients.reshape(frames, 256, 128), record.reshape(frames, HOP, cols), *tables,
    )
    return updated.reshape(coefficients.shape), residual.reshape(rows, cols)


def solution(mesh):
    return jax.shard_map(
        functools.partial(body, mesh.shape["chan"], mesh.shape["tm"]),
        mesh=mesh,
        in_specs=(P("tm", "chan"), P("tm", None, "chan", None), P(), P(), P()),
        out_specs=(P("tm", None, "chan", None), P("tm", "chan")),
        check_vma=False,
    )
```

profile of v0, /device:TPU:1, one launch (start us, length us, event | category | flops | bytes accessed | tf_op | source)
XLA Modules:
  0.0 121.2 jit_solution(17778988328082857175)
XLA Ops:
  1.3 0.0 copy-start
  1.3 1.6 %copy-done = f32[16,2,1,16384]{3,2,1,0:T(1,128)S(1)} copy-done((f32[16,2,1,16384]{3,2,1,0:T(1,128)S(1)}, f32[16,2,1,16384]{3,2,1,0:T(1,128)}, u32[]{:S(2)}) %copy-start) | copy-done | bytes 2097176
  2.9 0.0 copy-start.1
  2.9 0.9 copy-done.1
  3.8 0.0 copy-start.2
  3.8 0.9 copy-done.2
  4.8 0.0 copy-start.3
  4.8 0.9 copy-done.3
  5.7 0.0 copy-start.4
  5.7 0.9 copy-done.4
  6.7 0.0 copy-start.5
  6.7 0.9 copy-done.5
  7.6 0.0 copy-start.6
  7.6 0.8 copy-done.6
  8.4 0.0 copy-start.7
  8.4 0.8 copy-done.7
  9.3 0.7 copy-done.8
  9.9 0.0 copy-start.9
  9.9 0.7 copy-done.9
  10.6 105.7 %shard_map.131 = (f32[16,256,128]{2,1,0:T(8,128)S(1)}, f32[16,128,512]{2,1,0:T(8,128)}) custom-call(s32[1]{0:T(128)S(6)} %copy.17.start_ref, s32[32]{0:T(128)S(1)} %copy-done.8, f32[8]{0:T(128)S(1)} %copy-done.9, f32[16,256,128]{2,1,0:T(8,128)S(1)} %bitcast.5, f32[16,128,512]{2,1,0:T(8,128)} %bitcast.6, bf16[2,256,256]{2,1,0:T(8,128)(2,1)S(1)} %copy-done.4, ...), custom_call_target="tpu_custom_call" | custom-call | tf_op jit(solution)/shard_map/pallas_call | solution.py:269
  116.2 0.0 copy-start.10
  116.2 1.3 %copy.18 = f32[16,2,1,16384]{3,2,1,0:T(1,128)} copy(f32[16,2,1,16384]{3,2,1,0:T(1,128)S(1)} %bitcast.4) | data formatting | bytes 4194304
  117.6 1.6 %copy-done.10 = f32[16,128,512]{2,1,0:T(8,128)S(1)} copy-done((f32[16,128,512]{2,1,0:T(8,128)S(1)}, f32[16,128,512]{2,1,0:T(8,128)}, u32[]{:S(2)}) %copy-start.10) | copy-done | bytes 4194328
  119.2 2.0 %copy.19 = f32[2048,512]{1,0:T(8,128)} copy(f32[2048,512]{1,0:T(8,128)S(1)} %bitcast.7) | data formatting | bytes 8388608
  (1 shorter events, 0.0 us)
Async XLA Ops:
  1.3 1.6 %copy-start = (f32[16,2,1,16384]{3,2,1,0:T(1,128)S(1)}, f32[16,2,1,16384]{3,2,1,0:T(1,128)}, u32[]{:S(2)}) copy-start(f32[16,2,1,16384]{3,2,1,0:T(1,128)} %param.13) | copy-start | bytes 6291460
  2.9 0.9 copy-start.1
  3.8 0.9 copy-start.2
  4.8 0.9 copy-start.3
  5.7 0.9 copy-start.4
  6.7 0.9 copy-start.5
  7.6 0.8 copy-start.6
  8.4 0.8 copy-start.7
  9.3 0.7 copy-start.8
  9.9 0.7 copy-start.9
  116.2 2.9 %copy-start.10 = (f32[16,128,512]{2,1,0:T(8,128)S(1)}, f32[16,128,512]{2,1,0:T(8,128)}, u32[]{:S(2)}) copy-start(f32[16,128,512]{2,1,0:T(8,128)} %get-tuple-element.5) | copy-start | bytes 12582916
where the time goes:
time: 122 us; the launch traced here: 121 us
  Pallas kernels  106 us (87%)
  local copies, waits for them, and re-layouts  14.2 us (12%)
  between operations  1.31 us (1%)
    pallas_call x1, Pallas kernels, body(): pl.pallas_call(functools.partial(kernel, n_chan, n_tm), out_shape=(jax.Sh...  106 us
    unnamed x24, local copies, waits for them, and re-layouts  14.2 us

commit v1 on v0

--- a/solution.py
+++ b/solution.py
@@ -3,7 +3,6 @@
 
 import jax
 import jax.numpy as jnp
-import ml_dtypes
 import numpy as np
 from jax import lax
 from jax.experimental import pallas as pl
@@ -14,15 +13,11 @@
 HOP = 128
 NB = 32
 CHUNK = 4
+VMEM_LIMIT = 60 * 1024 * 1024
+PIECES = 8
 MESH = pl.DeviceIdType.MESH
 F32 = jnp.float32
 BF16 = jnp.bfloat16
-
-
-def halves_of(table):
-    high = table.astype(ml_dtypes.bfloat16)
-    low = (table - high.astype(np.float64)).astype(ml_dtypes.bfloat16)
-    return np.stack([high, low])
 
 
 def dft_tables(devices):
@@ -33,11 +28,10 @@
     inverse = np.block([[c, -s], [s, c]])
     per = side // devices
     order = [r * side + d * per + q for d in range(devices) for r in range(2) for q in range(per)]
-    first = inverse
     second = inverse[order]
     turn = 2.0 * math.pi * np.outer(idx, idx) / side**2
     twist = np.stack([np.cos(turn), np.sin(turn)]).astype(np.float32) / np.float32(side)
-    return halves_of(first), halves_of(second), halves_of(second.T), halves_of(first.T), twist
+    return np.stack([inverse, second, second.T, inverse.T]).astype(np.float32), twist
 
 
 def window_table():
@@ -57,11 +51,33 @@
     return dot(matrix[0], high) + (dot(matrix[0], low) + dot(matrix[1], high))
 
 
+def two_steps(matrices, k, twist, conj, pair):
+    side = 128
+    y = dot3(matrices.at[k], jnp.concatenate(pair, axis=1))
+    rows = []
+    for a in range(2):
+        yr, yi = y[:side, a * side:(a + 1) * side], y[side:, a * side:(a + 1) * side]
+        if conj:
+            tr, ti = yr * twist[0] + yi * twist[1], yi * twist[0] - yr * twist[1]
+        else:
+            tr, ti = yr * twist[0] - yi * twist[1], yr * twist[1] + yi * twist[0]
+        rows.append(jnp.concatenate([tr, ti], axis=1))
+    return dot3(matrices.at[k + 1], jnp.concatenate(rows, axis=0), True)
+
+
+def shrunk(coef, u, limit):
+    cr, ci = coef[:128] + u[:128], coef[128:] + u[128:]
+    m = jnp.sqrt(cr * cr + ci * ci)
+    factor = jnp.maximum(m - limit, 0.0) / jnp.maximum(m, limit)
+    return cr * factor, ci * factor
+
+
 def kernel(
     n_chan, n_tm,
-    start_ref, level_ref, levels_ref, coef_hbm, rec_hbm, first_ref, second_ref, back1_ref, back2_ref, twist_ref, window_ref, windowt_ref,
-    upd_hbm, res_hbm,
-    coef, rec, send_f, recv_f, send_b, recv_b, halo_s, halo_p, send_p, carry, synth, analy,
+    start_hbm, level_hbm, levels_hbm, coef_hbm, rec_hbm, tables_hbm, twist_hbm, window_hbm,
+    upd_hbm, res_hbm, last_hbm,
+    coef, rec, send_f, recv_f, send_b, recv_b, halo_s, halo_p, send_p, carry, synth, analy, tables, ahead, back, twist, window,
+    start_ref, level_ref, levels_ref,
     in_sem, out_sem, ssem_f, rsem_f, ssem_b, rsem_b, hsend, hrecv,
 ):
     me = lax.axis_index("chan")
@@ -71,10 +87,13 @@
     chunks = frames // CHUNK
     side = 128
 
-    load_coef = pltpu.make_async_copy(coef_hbm, coef, in_sem.at[0])
-    load_rec = pltpu.make_async_copy(rec_hbm, rec, in_sem.at[1])
-    load_coef.start()
-    load_rec.start()
+    early = [(tables_hbm, tables), (twist_hbm, twist),
+             (coef_hbm.at[frames - 1], coef.at[frames - 1]),
+             (coef_hbm.at[pl.ds(0, CHUNK - 1)], coef.at[pl.ds(0, CHUNK - 1)])]
+    later = [(coef_hbm.at[pl.ds(CHUNK - 1, frames - CHUNK)], coef.at[pl.ds(CHUNK - 1, frames - CHUNK)]),
+             (window_hbm, window), (start_hbm, start_ref), (level_hbm, level_ref), (levels_hbm, levels_ref),
+             (rec_hbm, rec)]
+    loads = [pltpu.make_async_copy(src, dst, in_sem.at[i]) for i, (src, dst) in enumerate(early + later)]
 
     barrier = pltpu.get_barrier_semaphore()
 
@@ -85,19 +104,13 @@
     lax.fori_loop(1, n_chan, greet, 0)
     for other in (before, after):
         pl.semaphore_signal(barrier, inc=1, device_id={"tm": other}, device_id_type=MESH)
+    for load in loads:
+        load.start()
 
     def forward(j):
         for pair in range(CHUNK // 2):
             q = j * CHUNK + 2 * pair
-            lanes = [coef[lax.rem(q + a + frames - 1, frames)] for a in range(2)]
-            y = dot3(first_ref, jnp.concatenate(lanes, axis=1))
-            rows = []
-            for a in range(2):
-                yr, yi = y[:side, a * side:(a + 1) * side], y[side:, a * side:(a + 1) * side]
-                tr = yr * twist_ref[0] - yi * twist_ref[1]
-                ti = yr * twist_ref[1] + yi * twist_ref[0]
-                rows.append(jnp.concatenate([tr, ti], axis=1))
-            x = dot3(second_ref, jnp.concatenate(rows, axis=0), True)
+            x = two_steps(ahead, 0, twist, False, [coef[lax.rem(q + a + frames - 1, frames)] for a in range(2)])
             for a in range(2):
                 send_f[j, 2 * pair + a] = x[:, a * side:(a + 1) * side]
 
@@ -122,7 +135,10 @@
     def wait_bytes(ref, sem):
         pltpu.make_async_copy(ref, ref, sem).wait()
 
-    load_coef.wait()
+    for load in loads[:len(early)]:
+        load.wait()
+    for k in range(2):
+        ahead[k, 0], ahead[k, 1] = split(tables[k])
     forward(0)
     pl.semaphore_wait(barrier, n_chan + 1)
     exchange(send_f, recv_f, ssem_f, rsem_f, 0)
@@ -132,6 +148,8 @@
         exchange(send_f, recv_f, ssem_f, rsem_f, j)
         return 0
 
+    for load in loads[len(early):-1]:
+        load.wait()
     lax.fori_loop(1, chunks, forward_step, 0)
 
     start = start_ref[0]
@@ -144,10 +162,13 @@
         phase = ((n_idx + later) * (start + (within >> 1)) + (within & 1) * (FRAME // 4)) & (FRAME - 1)
         return window * jnp.cos(phase.astype(F32) * (2.0 * math.pi / FRAME))
 
-    synth[0], synth[1] = split(2.0 * wave(0, window_ref[...]))
-    analy[0], analy[1] = split(wave(1, windowt_ref[...]))
+    synth[0], synth[1] = split(2.0 * wave(0, window[0]))
+    analy[0], analy[1] = split(wave(1, window[1]))
     carry[...] = jnp.zeros_like(carry)
-    load_rec.wait()
+    limit = levels_ref[level_ref[me]]
+    for k in range(2):
+        back[k, 0], back[k, 1] = split(tables[2 + k])
+    loads[-1].wait()
 
     def spectra(i, tile):
         q = lax.rem(i + 1, frames)
@@ -160,13 +181,13 @@
         rec[i, :, cols] = rest
         return dot3(analy, rest)
 
+    def store_residual(i):
+        pltpu.make_async_copy(rec.at[i], res_hbm.at[i], out_sem.at[0]).start()
+
     def put(i, tile, value, add=False):
         p = lax.rem(i + frames - 2, frames)
         where = (p // CHUNK, lax.rem(p, CHUNK), pl.ds(tile, 2 * NB, stride=4))
         send_b[where] = value + send_b[where] if add else value
-
-    def store_residual(i):
-        pltpu.make_async_copy(rec.at[i], res_hbm.at[i], out_sem.at[0]).start()
 
     def step(i, _):
         for h in range(2):
@@ -222,31 +243,18 @@
         put(0, k, jnp.where(t > 0, halo_p[:, cols], 0.0), True)
     exchange(send_b, recv_b, ssem_b, rsem_b, chunks - 1)
 
-    limit = levels_ref[level_ref[me]]
-
     def backward(j, _):
         wait_bytes(recv_b.at[j], rsem_b.at[j])
         for pair in range(CHUNK // 2):
-            y = dot3(back1_ref, jnp.concatenate([recv_b[j, 2 * pair], recv_b[j, 2 * pair + 1]], axis=1))
-            rows = []
-            for a in range(2):
-                yr, yi = y[:side, a * side:(a + 1) * side], y[side:, a * side:(a + 1) * side]
-                tr = yr * twist_ref[0] + yi * twist_ref[1]
-                ti = yi * twist_ref[0] - yr * twist_ref[1]
-                rows.append(jnp.concatenate([tr, ti], axis=1))
-            u = dot3(back2_ref, jnp.concatenate(rows, axis=0), True)
+            u = two_steps(back, 0, twist, True, [recv_b[j, 2 * pair], recv_b[j, 2 * pair + 1]])
             for a in range(2):
                 f = lax.rem(j * CHUNK + 2 * pair + a + 2, frames)
-                cr = coef[f, :side] + u[:side, a * side:(a + 1) * side]
-                ci = coef[f, side:] + u[side:, a * side:(a + 1) * side]
-                m = jnp.sqrt(cr * cr + ci * ci)
-                shrink = jnp.maximum(m - limit, 0.0) / jnp.maximum(m, limit)
-                coef[f, :side] = cr * shrink
-                coef[f, side:] = ci * shrink
-                pltpu.make_async_copy(coef.at[f], upd_hbm.at[f], out_sem.at[1]).start()
-        return 0
-
-    lax.fori_loop(0, chunks, backward, 0)
+                coef[f, :side], coef[f, side:] = shrunk(coef[f], u[:, a * side:(a + 1) * side], limit)
+        done = pl.ds(j * CHUNK + 2, CHUNK)
+        pltpu.make_async_copy(coef.at[done], upd_hbm.at[done], out_sem.at[1]).start()
+        return 0
+
+    lax.fori_loop(0, chunks - 1, backward, 0)
 
     def drain(j, _):
         for buf, sem in ((send_f, ssem_f), (send_b, ssem_b)):
@@ -255,7 +263,59 @@
 
     lax.fori_loop(0, chunks, drain, 0)
     wait_bytes(rec, out_sem.at[0])
-    wait_bytes(coef, out_sem.at[1])
+    wait_bytes(coef.at[pl.ds(0, frames - CHUNK)], out_sem.at[1])
+    wait_bytes(recv_b.at[chunks - 1], rsem_b.at[chunks - 1])
+    give = pltpu.make_async_copy(recv_b.at[chunks - 1], last_hbm, out_sem.at[2])
+    give.start()
+    give.wait()
+
+
+def finish(
+    level_hbm, levels_hbm, coef_hbm, tables_hbm, twist_hbm, last_hbm, upd1_hbm, res1_hbm,
+    upd_hbm, res_hbm,
+    last_b, coef, upd, rec, tables, back, twist, level_ref, levels_ref, in_sem, move_sem, out_sem,
+):
+    frames = coef_hbm.shape[0]
+    loads = [pltpu.make_async_copy(src, dst, in_sem.at[i]) for i, (src, dst) in enumerate([
+        (last_hbm, last_b), (tables_hbm.at[pl.ds(2, 2)], tables), (twist_hbm, twist),
+        (coef_hbm.at[pl.ds(frames - 2, 2)], coef.at[0]), (coef_hbm.at[pl.ds(0, 2)], coef.at[1]),
+        (level_hbm, level_ref), (levels_hbm, levels_ref)])]
+    moves, stores = [], []
+    spans = [(upd1_hbm, upd, upd_hbm, 2, frames - CHUNK)]
+    spans += [(res1_hbm, rec, res_hbm, i * frames // PIECES, frames // PIECES) for i in range(PIECES)]
+    for i, (src, via, dst, at, size) in enumerate(spans):
+        some = pl.ds(at, size)
+        moves.append((pltpu.make_async_copy(src.at[some], via.at[some], move_sem.at[i]),
+                      pltpu.make_async_copy(via.at[some], dst.at[some], out_sem.at[i])))
+    for load in loads:
+        load.start()
+    for load, _ in moves:
+        load.start()
+    for load in loads:
+        load.wait()
+    for k in range(2):
+        back[k, 0], back[k, 1] = split(tables[k])
+
+    def forward_moves(some):
+        for load, store in some:
+            load.wait()
+            store.start()
+            stores.append(store)
+
+    limit = levels_ref[level_ref[lax.axis_index("chan")]]
+    forward_moves(moves[:2])
+    for pair in range(CHUNK // 2):
+        u = two_steps(back, 0, twist, True, [last_b[2 * pair], last_b[2 * pair + 1]])
+        for a in range(2):
+            coef[pair, a, :128], coef[pair, a, 128:] = shrunk(coef[pair, a], u[:, a * 128:(a + 1) * 128], limit)
+        first = (frames - CHUNK + 2 * pair + 2) % frames
+        store = pltpu.make_async_copy(coef.at[pair], upd_hbm.at[pl.ds(first, 2)], out_sem.at[len(moves) + pair])
+        store.start()
+        stores.append(store)
+        if pair == 0:
+            forward_moves(moves[2:])
+    for store in stores:
+        store.wait()
 
 
 def body(n_chan, n_tm, record, coefficients, band_start, band_level, levels):
@@ -263,14 +323,22 @@
     frames = coefficients.shape[0]
     chunks = frames // CHUNK
     window = window_table()
-    tables = [jnp.asarray(x) for x in (*dft_tables(n_chan), window, window.T.copy())]
-    vmem, smem, hbm = (pl.BlockSpec(memory_space=m) for m in (pltpu.VMEM, pltpu.SMEM, pl.ANY))
+    tables, twist = dft_tables(n_chan)
+    constants = [jnp.asarray(x) for x in (tables, twist, np.stack([window, window.T]))]
+    hbm = pl.BlockSpec(memory_space=pl.ANY)
     block = pltpu.VMEM((chunks, CHUNK, 8 * n_chan, 128), F32)
-    updated, residual = pl.pallas_call(
+    coef_shape = jax.ShapeDtypeStruct((frames, 256, 128), F32)
+    rec_shape = jax.ShapeDtypeStruct((frames, HOP, cols), F32)
+    coef_in, rec_in = coefficients.reshape(frames, 256, 128), record.reshape(frames, HOP, cols)
+    upd1, res1, last_b = pl.pallas_call(
         functools.partial(kernel, n_chan, n_tm),
-        out_shape=(jax.ShapeDtypeStruct((frames, 256, 128), F32), jax.ShapeDtypeStruct((frames, HOP, cols), F32)),
-        in_specs=[smem] * 3 + [hbm] * 2 + [vmem] * len(tables),
-        out_specs=(hbm, hbm),
+        out_shape=(
+            coef_shape,
+            rec_shape,
+            jax.ShapeDtypeStruct((CHUNK, 8 * n_chan, 128), F32),
+        ),
+        in_specs=[hbm] * 8,
+        out_specs=(hbm,) * 3,
         scratch_shapes=[
             pltpu.VMEM((frames, 256, 128), F32),
             pltpu.VMEM((frames, HOP, cols), F32),
@@ -281,8 +349,16 @@
             pltpu.VMEM((2 * NB, cols), F32),
             pltpu.VMEM((2, 128, 128), BF16),
             pltpu.VMEM((2, 128, 128), BF16),
-            pltpu.SemaphoreType.DMA((2,)),
-            pltpu.SemaphoreType.DMA((2,)),
+            pltpu.VMEM((4, 256, 256), F32),
+            pltpu.VMEM((2, 2, 256, 256), BF16),
+            pltpu.VMEM((2, 2, 256, 256), BF16),
+            pltpu.VMEM((2, 128, 128), F32),
+            pltpu.VMEM((2, 128, 128), F32),
+            pltpu.SMEM(band_start.shape, jnp.int32),
+            pltpu.SMEM(band_level.shape, jnp.int32),
+            pltpu.SMEM(levels.shape, F32),
+            pltpu.SemaphoreType.DMA((10,)),
+            pltpu.SemaphoreType.DMA((3,)),
             pltpu.SemaphoreType.DMA((chunks,)),
             pltpu.SemaphoreType.DMA((chunks,)),
             pltpu.SemaphoreType.DMA((chunks,)),
@@ -291,12 +367,32 @@
             pltpu.SemaphoreType.DMA((2,)),
         ],
         compiler_params=pltpu.CompilerParams(
-            collective_id=0, has_side_effects=True, vmem_limit_bytes=48 * 1024 * 1024
+            collective_id=0, has_side_effects=True, vmem_limit_bytes=VMEM_LIMIT
         ),
     )(
-        band_start, band_level, levels,
-        coefficients.reshape(frames, 256, 128), record.reshape(frames, HOP, cols), *tables,
+        band_start, band_level, levels, coef_in, rec_in, *constants,
     )
+    updated, residual = pl.pallas_call(
+        finish,
+        out_shape=(coef_shape, rec_shape),
+        in_specs=[hbm] * 8,
+        out_specs=(hbm, hbm),
+        scratch_shapes=[
+            pltpu.VMEM((CHUNK, 8 * n_chan, 128), F32),
+            pltpu.VMEM((CHUNK // 2, 2, 256, 128), F32),
+            pltpu.VMEM((frames, 256, 128), F32),
+            pltpu.VMEM((frames, HOP, cols), F32),
+            pltpu.VMEM((2, 256, 256), F32),
+            pltpu.VMEM((2, 2, 256, 256), BF16),
+            pltpu.VMEM((2, 128, 128), F32),
+            pltpu.SMEM(band_level.shape, jnp.int32),
+            pltpu.SMEM(levels.shape, F32),
+            pltpu.SemaphoreType.DMA((7,)),
+            pltpu.SemaphoreType.DMA((PIECES + 1,)),
+            pltpu.SemaphoreType.DMA((PIECES + 1 + CHUNK // 2,)),
+        ],
+        compiler_params=pltpu.CompilerParams(vmem_limit_bytes=VMEM_LIMIT),
+    )(band_level, levels, coef_in, constants[0], constants[1], last_b, upd1, res1)
     return updated.reshape(coefficients.shape), residual.reshape(rows, cols)
 
 

time: 122 us -> 111 us (0.910)
  local copies, waits for them, and re-layouts: 14.2 us -> 0 us
  Pallas kernels: 106 us -> 109 us
    unnamed x24 -> x0, local copies, waits for them, and re-layouts: 14.2 us -> none
    pallas_call x1 -> x2, Pallas kernels: 106 us -> 109 us  [the longest x1 104 us: body(): pl.pallas_call(functools.partial(kernel, n_chan, n_tm), out_shape=(coef_s...]
where the time goes in v1:
time: 111 us
  Pallas kernels  109 us (98%)
  between operations  1.28 us (1%)
    pallas_call x1, Pallas kernels, body(): pl.pallas_call(functools.partial(kernel, n_chan, n_tm), out_shape=(coef_s...  104 us
    pallas_call x1, Pallas kernels, body(): pl.pallas_call(finish, out_shape=(coef_shape, rec_shape), in_specs=[hbm]...  5.67 us

profile of v1, /device:TPU:1, one launch (start us, length us, event | category | flops | bytes accessed | tf_op | source)
XLA Modules:
  0.0 110.7 jit_solution(13442669145455905301)
XLA Ops:
  1.3 103.7 %shard_map.95 = (f32[16,256,128]{2,1,0:T(8,128)}, f32[16,128,512]{2,1,0:T(8,128)}, f32[4,256,128]{2,1,0:T(8,128)}) custom-call(s32[1]{0:T(128)S(6)} %copy.11.start_hbm, s32[32]{0:T(128)} %level_hbm.3, f32[8]{0:T(128)} %levels_hbm.3, f32[16,256,128]{2,1,0:T(8,128)} %bitcast.4, f32[16,128,512]{2,1,0:T(8,128)} %bitcast.6, ...), custom_call_target="tpu_custom_call" | custom-call | tf_op jit(solution)/shard_map/pallas_call | solution.py:333
  105.0 5.7 %shard_map.96 = (f32[16,256,128]{2,1,0:T(8,128)}, f32[16,128,512]{2,1,0:T(8,128)}) custom-call(s32[32]{0:T(128)} %level_hbm.3, f32[8]{0:T(128)} %levels_hbm.3, f32[16,256,128]{2,1,0:T(8,128)} %bitcast.5, f32[4,256,256]{2,1,0:T(8,128)} %constant.6.clone.tables_hbm, f32[2,128,128]{2,1,0:T(8,128)} %constant.7.clone.twist_hbm, ...), custom_call_target="tpu_custom_call" | custom-call | tf_op jit(solution)/shard_map/pallas_call | solution.py:375

commit v2 on v1

--- a/solution.py
+++ b/solution.py
@@ -13,8 +13,7 @@
 HOP = 128
 NB = 32
 CHUNK = 4
-VMEM_LIMIT = 60 * 1024 * 1024
-PIECES = 8
+VMEM_LIMIT = 40 * 1024 * 1024
 MESH = pl.DeviceIdType.MESH
 F32 = jnp.float32
 BF16 = jnp.bfloat16
@@ -75,10 +74,10 @@
 def kernel(
     n_chan, n_tm,
     start_hbm, level_hbm, levels_hbm, coef_hbm, rec_hbm, tables_hbm, twist_hbm, window_hbm,
-    upd_hbm, res_hbm, last_hbm,
-    coef, rec, send_f, recv_f, send_b, recv_b, halo_s, halo_p, send_p, carry, synth, analy, tables, ahead, back, twist, window,
+    coef, rec, last_b, back, twist, limits,
+    send_f, recv_f, send_b, recv_b, halo_s, halo_p, send_p, carry, synth, analy, tables, ahead, window,
     start_ref, level_ref, levels_ref,
-    in_sem, out_sem, ssem_f, rsem_f, ssem_b, rsem_b, hsend, hrecv,
+    in_sem, ssem_f, rsem_f, ssem_b, rsem_b, hsend, hrecv,
 ):
     me = lax.axis_index("chan")
     t = lax.axis_index("tm")
@@ -117,8 +116,7 @@
     def exchange(src, dst, ssem, rsem, j):
         mine = pl.ds(pl.multiple_of(me * 8, 8), 8)
 
-        def one(i, _):
-            d = lax.rem(me + i, n_chan)
+        def send(d):
             pltpu.make_async_remote_copy(
                 src_ref=src.at[j, :, pl.ds(pl.multiple_of(d * 8, 8), 8)],
                 dst_ref=dst.at[j, :, mine],
@@ -127,9 +125,14 @@
                 device_id={"chan": d},
                 device_id_type=MESH,
             ).start()
+
+        def both(i, _):
+            send(lax.rem(me + i, n_chan))
+            send(lax.rem(me + n_chan - i, n_chan))
             return 0
 
-        lax.fori_loop(1, n_chan, one, 0)
+        lax.fori_loop(1, n_chan // 2, both, 0)
+        send(lax.rem(me + n_chan // 2, n_chan))
         pltpu.make_async_copy(src.at[j, :, mine], dst.at[j, :, mine], rsem.at[j]).start()
 
     def wait_bytes(ref, sem):
@@ -166,6 +169,7 @@
     analy[0], analy[1] = split(wave(1, window[1]))
     carry[...] = jnp.zeros_like(carry)
     limit = levels_ref[level_ref[me]]
+    limits[...] = jnp.full(limits.shape, limit, F32)
     for k in range(2):
         back[k, 0], back[k, 1] = split(tables[2 + k])
     loads[-1].wait()
@@ -180,9 +184,6 @@
         rest = rec[i, :, cols] - est
         rec[i, :, cols] = rest
         return dot3(analy, rest)
-
-    def store_residual(i):
-        pltpu.make_async_copy(rec.at[i], res_hbm.at[i], out_sem.at[0]).start()
 
     def put(i, tile, value, add=False):
         p = lax.rem(i + frames - 2, frames)
@@ -198,7 +199,6 @@
             carry[:, cols] = part[2 * NB:]
             for a, k in enumerate(tiles):
                 put(i, k, analysed[:, a * side:(a + 1) * side])
-        store_residual(i)
         return 0
 
     wait_bytes(recv_f.at[0], rsem_f.at[0])
@@ -224,7 +224,6 @@
         send_p[:, h * 256:(h + 1) * 256] = part[2 * NB:]
         for a, k in enumerate(tiles):
             put(last, k, part[:2 * NB, a * side:(a + 1) * side])
-    store_residual(last)
     part_out = pltpu.make_async_remote_copy(
         src_ref=send_p, dst_ref=halo_p, send_sem=hsend.at[1], recv_sem=hrecv.at[1],
         device_id={"tm": after}, device_id_type=MESH)
@@ -250,8 +249,6 @@
             for a in range(2):
                 f = lax.rem(j * CHUNK + 2 * pair + a + 2, frames)
                 coef[f, :side], coef[f, side:] = shrunk(coef[f], u[:, a * side:(a + 1) * side], limit)
-        done = pl.ds(j * CHUNK + 2, CHUNK)
-        pltpu.make_async_copy(coef.at[done], upd_hbm.at[done], out_sem.at[1]).start()
         return 0
 
     lax.fori_loop(0, chunks - 1, backward, 0)
@@ -262,58 +259,26 @@
         return 0
 
     lax.fori_loop(0, chunks, drain, 0)
-    wait_bytes(rec, out_sem.at[0])
-    wait_bytes(coef.at[pl.ds(0, frames - CHUNK)], out_sem.at[1])
     wait_bytes(recv_b.at[chunks - 1], rsem_b.at[chunks - 1])
-    give = pltpu.make_async_copy(recv_b.at[chunks - 1], last_hbm, out_sem.at[2])
-    give.start()
-    give.wait()
-
-
-def finish(
-    level_hbm, levels_hbm, coef_hbm, tables_hbm, twist_hbm, last_hbm, upd1_hbm, res1_hbm,
-    upd_hbm, res_hbm,
-    last_b, coef, upd, rec, tables, back, twist, level_ref, levels_ref, in_sem, move_sem, out_sem,
-):
-    frames = coef_hbm.shape[0]
-    loads = [pltpu.make_async_copy(src, dst, in_sem.at[i]) for i, (src, dst) in enumerate([
-        (last_hbm, last_b), (tables_hbm.at[pl.ds(2, 2)], tables), (twist_hbm, twist),
-        (coef_hbm.at[pl.ds(frames - 2, 2)], coef.at[0]), (coef_hbm.at[pl.ds(0, 2)], coef.at[1]),
-        (level_hbm, level_ref), (levels_hbm, levels_ref)])]
-    moves, stores = [], []
-    spans = [(upd1_hbm, upd, upd_hbm, 2, frames - CHUNK)]
-    spans += [(res1_hbm, rec, res_hbm, i * frames // PIECES, frames // PIECES) for i in range(PIECES)]
-    for i, (src, via, dst, at, size) in enumerate(spans):
-        some = pl.ds(at, size)
-        moves.append((pltpu.make_async_copy(src.at[some], via.at[some], move_sem.at[i]),
-                      pltpu.make_async_copy(via.at[some], dst.at[some], out_sem.at[i])))
-    for load in loads:
-        load.start()
-    for load, _ in moves:
-        load.start()
-    for load in loads:
-        load.wait()
-    for k in range(2):
-        back[k, 0], back[k, 1] = split(tables[k])
-
-    def forward_moves(some):
-        for load, store in some:
-            load.wait()
-            store.start()
-            stores.append(store)
-
-    limit = levels_ref[level_ref[lax.axis_index("chan")]]
-    forward_moves(moves[:2])
+    last_b[...] = recv_b[chunks - 1]
+
+
+def finish(coef, rec, last_b, back, twist, limits, upd_hbm, res_hbm, out, sem):
+    frames = coef.shape[0]
+    stores = [pltpu.make_async_copy(coef.at[pl.ds(2, frames - CHUNK)], upd_hbm.at[pl.ds(2, frames - CHUNK)], sem.at[0])]
+    half = frames // 2
+    for i in range(2):
+        stores.append(pltpu.make_async_copy(rec.at[pl.ds(i * half, half)], res_hbm.at[pl.ds(i * half, half)], sem.at[1 + i]))
+    for store in stores:
+        store.start()
     for pair in range(CHUNK // 2):
         u = two_steps(back, 0, twist, True, [last_b[2 * pair], last_b[2 * pair + 1]])
+        first = (frames - CHUNK + 2 * pair + 2) % frames
         for a in range(2):
-            coef[pair, a, :128], coef[pair, a, 128:] = shrunk(coef[pair, a], u[:, a * 128:(a + 1) * 128], limit)
-        first = (frames - CHUNK + 2 * pair + 2) % frames
-        store = pltpu.make_async_copy(coef.at[pair], upd_hbm.at[pl.ds(first, 2)], out_sem.at[len(moves) + pair])
+            out[pair, a, :128], out[pair, a, 128:] = shrunk(coef[first + a], u[:, a * 128:(a + 1) * 128], limits[...][:1])
+        store = pltpu.make_async_copy(out.at[pair], upd_hbm.at[pl.ds(first, 2)], sem.at[3 + pair])
         store.start()
         stores.append(store)
-        if pair == 0:
-            forward_moves(moves[2:])
     for store in stores:
         store.wait()
 
@@ -325,23 +290,23 @@
     window = window_table()
     tables, twist = dft_tables(n_chan)
     constants = [jnp.asarray(x) for x in (tables, twist, np.stack([window, window.T]))]
-    hbm = pl.BlockSpec(memory_space=pl.ANY)
+    vmem, hbm = (pl.BlockSpec(memory_space=m) for m in (pltpu.VMEM, pltpu.HBM))
     block = pltpu.VMEM((chunks, CHUNK, 8 * n_chan, 128), F32)
     coef_shape = jax.ShapeDtypeStruct((frames, 256, 128), F32)
     rec_shape = jax.ShapeDtypeStruct((frames, HOP, cols), F32)
-    coef_in, rec_in = coefficients.reshape(frames, 256, 128), record.reshape(frames, HOP, cols)
-    upd1, res1, last_b = pl.pallas_call(
+    parts = pl.pallas_call(
         functools.partial(kernel, n_chan, n_tm),
         out_shape=(
-            coef_shape,
-            rec_shape,
-            jax.ShapeDtypeStruct((CHUNK, 8 * n_chan, 128), F32),
+            pltpu.VMEM((frames, 256, 128), F32),
+            pltpu.VMEM((frames, HOP, cols), F32),
+            pltpu.VMEM((CHUNK, 8 * n_chan, 128), F32),
+            pltpu.VMEM((2, 2, 256, 256), BF16),
+            pltpu.VMEM((2, 128, 128), F32),
+            pltpu.VMEM((8, 128), F32),
         ),
         in_specs=[hbm] * 8,
-        out_specs=(hbm,) * 3,
+        out_specs=(vmem,) * 6,
         scratch_shapes=[
-            pltpu.VMEM((frames, 256, 128), F32),
-            pltpu.VMEM((frames, HOP, cols), F32),
             block, block, block, block,
             pltpu.VMEM((8 * n_chan, 128), F32),
             pltpu.VMEM((2 * NB, cols), F32),
@@ -351,14 +316,11 @@
             pltpu.VMEM((2, 128, 128), BF16),
             pltpu.VMEM((4, 256, 256), F32),
             pltpu.VMEM((2, 2, 256, 256), BF16),
-            pltpu.VMEM((2, 2, 256, 256), BF16),
-            pltpu.VMEM((2, 128, 128), F32),
             pltpu.VMEM((2, 128, 128), F32),
             pltpu.SMEM(band_start.shape, jnp.int32),
             pltpu.SMEM(band_level.shape, jnp.int32),
             pltpu.SMEM(levels.shape, F32),
             pltpu.SemaphoreType.DMA((10,)),
-            pltpu.SemaphoreType.DMA((3,)),
             pltpu.SemaphoreType.DMA((chunks,)),
             pltpu.SemaphoreType.DMA((chunks,)),
             pltpu.SemaphoreType.DMA((chunks,)),
@@ -370,29 +332,19 @@
             collective_id=0, has_side_effects=True, vmem_limit_bytes=VMEM_LIMIT
         ),
     )(
-        band_start, band_level, levels, coef_in, rec_in, *constants,
+        band_start, *(pltpu.with_memory_space_constraint(x, pltpu.HBM) for x in (
+            band_level, levels,
+            coefficients.reshape(frames, 256, 128), record.reshape(frames, HOP, cols), *constants,
+        ))
     )
     updated, residual = pl.pallas_call(
         finish,
         out_shape=(coef_shape, rec_shape),
-        in_specs=[hbm] * 8,
+        in_specs=[vmem] * 6,
         out_specs=(hbm, hbm),
-        scratch_shapes=[
-            pltpu.VMEM((CHUNK, 8 * n_chan, 128), F32),
-            pltpu.VMEM((CHUNK // 2, 2, 256, 128), F32),
-            pltpu.VMEM((frames, 256, 128), F32),
-            pltpu.VMEM((frames, HOP, cols), F32),
-            pltpu.VMEM((2, 256, 256), F32),
-            pltpu.VMEM((2, 2, 256, 256), BF16),
-            pltpu.VMEM((2, 128, 128), F32),
-            pltpu.SMEM(band_level.shape, jnp.int32),
-            pltpu.SMEM(levels.shape, F32),
-            pltpu.SemaphoreType.DMA((7,)),
-            pltpu.SemaphoreType.DMA((PIECES + 1,)),
-            pltpu.SemaphoreType.DMA((PIECES + 1 + CHUNK // 2,)),
-        ],
+        scratch_shapes=[pltpu.VMEM((CHUNK // 2, 2, 256, 128), F32), pltpu.SemaphoreType.DMA((5,))],
         compiler_params=pltpu.CompilerParams(vmem_limit_bytes=VMEM_LIMIT),
-    )(band_level, levels, coef_in, constants[0], constants[1], last_b, upd1, res1)
+    )(*(pltpu.with_memory_space_constraint(x, pltpu.VMEM) for x in parts))
     return updated.reshape(coefficients.shape), residual.reshape(rows, cols)
 
 

time: 111 us -> 107 us (0.964)
  Pallas kernels: 109 us -> 106 us
    pallas_call x2, Pallas kernels: 109 us -> 106 us  [the longest x1 103 us: body(): pl.pallas_call(functools.partial(kernel, n_chan, n_tm), out_shape=(pltpu....]
where the time goes in v2:
time: 107 us
  Pallas kernels  106 us (99%)
  between operations  1.28 us (1%)
    pallas_call x1, Pallas kernels, body(): pl.pallas_call(functools.partial(kernel, n_chan, n_tm), out_shape=(pltpu....  103 us
    pallas_call x1, Pallas kernels, body(): pl.pallas_call(finish, out_shape=(coef_shape, rec_shape), in_specs=[vmem]...  2.73 us

profile of v2, /device:TPU:1, one launch (start us, length us, event | category | flops | bytes accessed | tf_op | source)
XLA Modules:
  0.0 107.0 jit_solution(17528511318010788592)
XLA Ops:
  1.3 102.9 %shard_map.95 = (f32[16,256,128]{2,1,0:T(8,128)S(1)}, f32[16,128,512]{2,1,0:T(8,128)S(1)}, f32[4,256,128]{2,1,0:T(8,128)S(1)}, bf16[2,2,256,256]{3,2,1,0:T(8,128...) custom-call(s32[1]{0:T(128)S(6)} %copy.11.start_hbm, s32[32]{0:T(128)} %level_hbm.1, f32[8]{0:T(128)} %levels_hbm.1, ...), custom_call_target="tpu_custom_call" | custom-call | tf_op jit(solution)/shard_map/pallas_call | solution.py:297
  104.2 2.7 %shard_map.96 = (f32[16,256,128]{2,1,0:T(8,128)}, f32[16,128,512]{2,1,0:T(8,128)}) custom-call(f32[16,256,128]{2,1,0:T(8,128)S(1)} %get-tuple-element.10.coef, f32[16,128,512]{2,1,0:T(8,128)S(1)} %get-tuple-element.11.rec, f32[4,256,128]{2,1,0:T(8,128)S(1)} %get-tuple-element.12.last_b, bf16[2,2,256,256]{3,2,1,0:T(8,128)(2,1)S(1)} %get-tuple-element.13.back, ...), custom_call_target="tpu_custom_call" | custom-call | tf_op jit(solution)/shard_map/pallas_call | solution.py:340

commit v3 on v2

--- a/solution.py
+++ b/solution.py
@@ -96,13 +96,14 @@
 
     barrier = pltpu.get_barrier_semaphore()
 
+    for other in (before, after):
+        pl.semaphore_signal(barrier, inc=1, device_id={"tm": other}, device_id_type=MESH)
+
     def greet(i, _):
         pl.semaphore_signal(barrier, inc=1, device_id={"chan": lax.rem(me + i, n_chan)}, device_id_type=MESH)
         return 0
 
     lax.fori_loop(1, n_chan, greet, 0)
-    for other in (before, after):
-        pl.semaphore_signal(barrier, inc=1, device_id={"tm": other}, device_id_type=MESH)
     for load in loads:
         load.start()
 

time: 107 us -> 107 us (level)
  no operation moved by 1% of the time
where the time goes in v3:
time: 107 us; the launch traced here: 106 us
  Pallas kernels  105 us (98%)
  between operations  1.28 us (1%)
    pallas_call x1, Pallas kernels, body(): pl.pallas_call(functools.partial(kernel, n_chan, n_tm), out_shape=(pltpu....  102 us
    pallas_call x1, Pallas kernels, body(): pl.pallas_call(finish, out_shape=(coef_shape, rec_shape), in_specs=[vmem]...  2.73 us

profile of v3, /device:TPU:1, one launch (start us, length us, event | category | flops | bytes accessed | tf_op | source)
XLA Modules:
  0.0 106.4 jit_solution(1178644489884594626)
XLA Ops:
  1.3 102.4 %shard_map.95 = (f32[16,256,128]{2,1,0:T(8,128)S(1)}, f32[16,128,512]{2,1,0:T(8,128)S(1)}, f32[4,256,128]{2,1,0:T(8,128)S(1)}, bf16[2,2,256,256]{3,2,1,0:T(8,128...) custom-call(s32[1]{0:T(128)S(6)} %copy.11.start_hbm, s32[32]{0:T(128)} %level_hbm.1, f32[8]{0:T(128)} %levels_hbm.1, ...), custom_call_target="tpu_custom_call" | custom-call | tf_op jit(solution)/shard_map/pallas_call | solution.py:298
  103.7 2.7 %shard_map.96 = (f32[16,256,128]{2,1,0:T(8,128)}, f32[16,128,512]{2,1,0:T(8,128)}) custom-call(f32[16,256,128]{2,1,0:T(8,128)S(1)} %get-tuple-element.10.coef, f32[16,128,512]{2,1,0:T(8,128)S(1)} %get-tuple-element.11.rec, f32[4,256,128]{2,1,0:T(8,128)S(1)} %get-tuple-element.12.last_b, bf16[2,2,256,256]{3,2,1,0:T(8,128)(2,1)S(1)} %get-tuple-element.13.back, ...), custom_call_target="tpu_custom_call" | custom-call | tf_op jit(solution)/shard_map/pallas_call | solution.py:341

commit v4 on v3

--- a/solution.py
+++ b/solution.py
@@ -99,11 +99,16 @@
     for other in (before, after):
         pl.semaphore_signal(barrier, inc=1, device_id={"tm": other}, device_id_type=MESH)
 
-    def greet(i, _):
-        pl.semaphore_signal(barrier, inc=1, device_id={"chan": lax.rem(me + i, n_chan)}, device_id_type=MESH)
-        return 0
-
-    lax.fori_loop(1, n_chan, greet, 0)
+    def greet(offset):
+        pl.semaphore_signal(barrier, inc=1, device_id={"chan": lax.rem(me + offset, n_chan)}, device_id_type=MESH)
+
+    def greet_both(i, _):
+        greet(n_chan // 2 - i)
+        greet(n_chan // 2 + i)
+        return 0
+
+    greet(n_chan // 2)
+    lax.fori_loop(1, n_chan // 2, greet_both, 0)
     for load in loads:
         load.start()
 

time: 107 us -> 107 us (level)
  no operation moved by 1% of the time
where the time goes in v4:
time: 107 us; the launch traced here: 106 us
  Pallas kernels  105 us (98%)
  between operations  1.28 us (1%)
    pallas_call x1, Pallas kernels, body(): pl.pallas_call(functools.partial(kernel, n_chan, n_tm), out_shape=(pltpu....  102 us
    pallas_call x1, Pallas kernels, body(): pl.pallas_call(finish, out_shape=(coef_shape, rec_shape), in_specs=[vmem]...  2.73 us

profile of v4, /device:TPU:1, one launch (start us, length us, event | category | flops | bytes accessed | tf_op | source)
XLA Modules:
  0.0 106.4 jit_solution(17647380286423022309)
XLA Ops:
  1.3 102.4 %shard_map.95 = (f32[16,256,128]{2,1,0:T(8,128)S(1)}, f32[16,128,512]{2,1,0:T(8,128)S(1)}, f32[4,256,128]{2,1,0:T(8,128)S(1)}, bf16[2,2,256,256]{3,2,1,0:T(8,128...) custom-call(s32[1]{0:T(128)S(6)} %copy.11.start_hbm, s32[32]{0:T(128)} %level_hbm.1, f32[8]{0:T(128)} %levels_hbm.1, ...), custom_call_target="tpu_custom_call" | custom-call | tf_op jit(solution)/shard_map/pallas_call | solution.py:303
  103.7 2.7 %shard_map.96 = (f32[16,256,128]{2,1,0:T(8,128)}, f32[16,128,512]{2,1,0:T(8,128)}) custom-call(f32[16,256,128]{2,1,0:T(8,128)S(1)} %get-tuple-element.10.coef, f32[16,128,512]{2,1,0:T(8,128)S(1)} %get-tuple-element.11.rec, f32[4,256,128]{2,1,0:T(8,128)S(1)} %get-tuple-element.12.last_b, bf16[2,2,256,256]{3,2,1,0:T(8,128)(2,1)S(1)} %get-tuple-element.13.back, ...), custom_call_target="tpu_custom_call" | custom-call | tf_op jit(solution)/shard_map/pallas_call | solution.py:346
